TPU v7x, 32 devices: a whole 2x2x4 slice. The times are simulated.
32 devices in a mesh: section: 8 (over z, x), dp: 4 (over y, core).
Axes of the slice: x: 2, y: 2, z: 4, core: 2. Of those that a mesh axis runs over, the one named last changes fastest.
Arguments:
- clip_pool: bfloat16 [16, 3, 4, 2, 640], P('dp'), may hold values from -6 to 6
- sample_ids: int32 [32], P('dp'), may hold values from 0 to 3
- timesteps: int32 [32], P('dp'), may hold values from 0 to 999
- noise_draw: bfloat16 [32, 3, 4, 2, 640], P('dp'), may hold values from -6 to 6
- keep_lists: int32 [32, 16], P('dp'), may hold values 0 or 1
- enc_weight: bfloat16 [8, 5760, 640], P('section'), may hold values from -0.078125 to 0.078125
- enc_gain: float32 [8, 640], P('section'), may hold values from 0.1 to 1.9
- dec_weight: bfloat16 [8, 1920, 640], P('section'), may hold values from -0.125 to 0.125
- dec_gain: float32 [8, 640], P('section'), may hold values from 0.1 to 1.9
Outputs:
- enc_weight_grad: float32 [8, 5760, 640], P('section', 'dp')
- enc_gain_grad: float32 [8, 640], P('section', 'dp')
- dec_weight_grad: float32 [8, 1920, 640], P('section', 'dp')
- dec_gain_grad: float32 [8, 640], P('section', 'dp')
All inputs are finite; a program needn't handle non-finite values. No bound on the sum of `keep_lists` on one device may be relied on, other than what follows from the above.
Results may differ from a plain program's by a relative error of at most 0.025.
Values may be sent and summed in bfloat16 or wider, within the bound.
No kernel may reach another device: no remote copies, remote signals or barrier semaphores. Data moves between devices by JAX's collectives and lax.ppermute only.
A program may use at most 64 MiB of HBM per device.

v0:
```python
import math

import jax
import jax.numpy as jnp
from jax import lax
from jax.sharding import PartitionSpec as P

GROUPS = 32


def from_behind(value, axis, by):
    length = lax.axis_size(axis)
    return lax.ppermute(value, axis, [(i, (i + by) % length) for i in range(length)])


def swapped(value, axis, apart):
    mask = 2**apart
    pairs = [(source, source ^ mask) for source in range(lax.axis_size(axis))]
    return lax.ppermute(value, axis, pairs)


def shifted(value, axis, steps):
    count = lax.axis_size(axis)
    first, last = (max(0, -steps), min(count, count - steps))
    return lax.ppermute(value, axis, [(source, source + steps) for source in range(first, last)])


def noise_level(timesteps):
    phase_arg = (timesteps.astype(jnp.float32) / 1000.0 + 0.008) / 1.008
    return jnp.cos(phase_arg * (math.pi / 2.0)) ** 2


def norm_act(values, gain_rows):
    batch_size = values.shape[0]
    channels = values.shape[-1]
    grouped = values.reshape(batch_size, -1, GROUPS, channels // GROUPS)
    center = grouped - jnp.mean(grouped, axis=(1, 3), keepdims=True)
    spread = jnp.mean(center * center, axis=(1, 3), keepdims=True)
    normed = (center * lax.rsqrt(spread + 1e-05)).reshape(values.shape)
    return jax.nn.silu(normed * gain_rows[:, None, None, None, :])


def spatial_columns(activation):
    grid_height = activation.shape[2]
    grid_width = activation.shape[3]
    padded = jnp.pad(activation, ((0, 0), (0, 0), (1, 1), (1, 1), (0, 0)))
    pieces = [
        padded[:, :, row_shift : row_shift + grid_height, col_shift : col_shift + grid_width, :]
        for row_shift in range(3)
        for col_shift in range(3)
    ]
    return jnp.concatenate(pieces, axis=-1).reshape(-1, 9 * activation.shape[-1])


def spatial_spread(columns, full_shape):
    batch_size, frames, grid_height, grid_width, channels = full_shape
    columns = columns.reshape(batch_size, frames, grid_height, grid_width, 9, channels)
    summed = jnp.zeros((batch_size, frames, grid_height + 2, grid_width + 2, channels), jnp.float32)
    for kernel_tap in range(9):
        row_shift = kernel_tap // 3
        col_shift = kernel_tap % 3
        summed = summed + jnp.pad(
            columns[:, :, :, :, kernel_tap, :],
            ((0, 0), (0, 0), (row_shift, 2 - row_shift), (col_shift, 2 - col_shift), (0, 0)),
        )
    return summed[:, :, 1 : grid_height + 1, 1 : grid_width + 1, :]


def temporal_columns(activation):
    frames = activation.shape[1]
    padded = jnp.pad(activation, ((0, 0), (1, 1), (0, 0), (0, 0), (0, 0)))
    pieces = [padded[:, frame_shift : frame_shift + frames] for frame_shift in range(3)]
    return jnp.concatenate(pieces, axis=-1).reshape(-1, 3 * activation.shape[-1])


def temporal_spread(columns, full_shape):
    batch_size, frames, grid_height, grid_width, channels = full_shape
    columns = columns.reshape(batch_size, frames, grid_height, grid_width, 3, channels)
    summed = jnp.zeros((batch_size, frames + 2, grid_height, grid_width, channels), jnp.float32)
    for kernel_tap in range(3):
        summed = summed + jnp.pad(
            columns[:, :, :, :, kernel_tap, :],
            ((0, 0), (kernel_tap, 2 - kernel_tap), (0, 0), (0, 0), (0, 0)),
        )
    return summed[:, 1 : frames + 1]


def gate_shape(keep_rate):
    return keep_rate[:, None, None, None, None]


def encoder_forward(stream, weight, gain_rows, keep_rate):
    activation = norm_act(stream.astype(jnp.float32), gain_rows).astype(jnp.bfloat16)
    branch = jnp.dot(spatial_columns(activation), weight, preferred_element_type=jnp.float32)
    return (
        stream.astype(jnp.float32) + gate_shape(keep_rate) * branch.reshape(stream.shape)
    ).astype(jnp.bfloat16)


def encoder_backward(stream, upstream, weight, gain_rows, keep_rate):
    activation, pullback = jax.vjp(norm_act, stream.astype(jnp.float32), gain_rows)
    gated = (gate_shape(keep_rate) * upstream.astype(jnp.float32)).astype(jnp.bfloat16)
    back_cols = lax.dot_general(
        gated.reshape(-1, stream.shape[-1]),
        weight,
        (((1,), (1,)), ((), ())),
        preferred_element_type=jnp.float32,
    )
    norm_grad, gain_grad = pullback(spatial_spread(back_cols, stream.shape))
    stream_grad = (upstream.astype(jnp.float32) + norm_grad).astype(jnp.bfloat16)
    return (stream_grad, activation.astype(jnp.bfloat16), gated, gain_grad)


def decoder_forward(stream, skip_act, weight, gain_rows, keep_rate):
    merged = stream.astype(jnp.float32) + skip_act.astype(jnp.float32)
    activation = norm_act(merged, gain_rows).astype(jnp.bfloat16)
    branch = jnp.dot(temporal_columns(activation), weight, preferred_element_type=jnp.float32)
    return (
        stream.astype(jnp.float32) + gate_shape(keep_rate) * branch.reshape(stream.shape)
    ).astype(jnp.bfloat16)


def decoder_backward(stream, skip_act, upstream, weight, gain_rows, keep_rate):
    merged = stream.astype(jnp.float32) + skip_act.astype(jnp.float32)
    activation, pullback = jax.vjp(norm_act, merged, gain_rows)
    gated = (gate_shape(keep_rate) * upstream.astype(jnp.float32)).astype(jnp.bfloat16)
    back_cols = lax.dot_general(
        gated.reshape(-1, stream.shape[-1]),
        weight,
        (((1,), (1,)), ((), ())),
        preferred_element_type=jnp.float32,
    )
    merged_grad, gain_grad = pullback(temporal_spread(back_cols, stream.shape))
    stream_grad = (upstream.astype(jnp.float32) + merged_grad).astype(jnp.bfloat16)
    return (
        stream_grad,
        merged_grad.astype(jnp.bfloat16),
        activation.astype(jnp.bfloat16),
        gated,
        gain_grad,
    )


def weight_term(columns, gated):
    return lax.dot_general(
        columns, gated, (((0,), (0,)), ((), ())), preferred_element_type=jnp.float32
    )


def pick(stack, index):
    return lax.dynamic_slice_in_dim(stack, index, 1, 0)


def place(stack, piece, index, active):
    return jnp.where(active, lax.dynamic_update_slice_in_dim(stack, piece, index, 0), stack)


def body(
    clip_pool,
    sample_ids,
    timesteps,
    noise_draw,
    keep_lists,
    enc_weight,
    enc_gain,
    dec_weight,
    dec_gain,
):
    sections = lax.axis_size("section")
    own_level = lax.axis_index("section")
    micro_count = noise_draw.shape[0]
    channels = noise_draw.shape[-1]
    loop_len = sections + micro_count - 1
    last_level = sections - 1
    bit_count = sections.bit_length() - 1
    enc_kernel = enc_weight[0]
    dec_kernel = dec_weight[0]
    keep_rates = keep_lists.astype(jnp.float32)
    enc_keep = lax.dynamic_slice_in_dim(keep_rates, own_level, 1, 1)[:, 0]
    dec_keep = lax.dynamic_slice_in_dim(keep_rates, own_level + sections, 1, 1)[:, 0]
    clean = jnp.take(clip_pool, sample_ids, axis=0).astype(jnp.float32)
    level_noise = noise_level(timesteps)[:, None, None, None, None]
    inputs = (
        jnp.sqrt(level_noise) * clean + jnp.sqrt(1.0 - level_noise) * noise_draw.astype(jnp.float32)
    ).astype(jnp.bfloat16)
    blank = jnp.zeros((1,) + noise_draw.shape[1:], jnp.bfloat16)
    store_blank = jnp.zeros(noise_draw.shape, jnp.bfloat16)

    def slot_of(item_index):
        active = (item_index >= 0) & (item_index < micro_count)
        return (active, jnp.clip(item_index, 0, micro_count - 1))

    def encoder_step(step_index, loop_state):
        incoming, enc_inputs, enc_outputs, bottom = loop_state
        active, slot_index = slot_of(step_index - own_level)
        given = jnp.where(own_level == 0, pick(inputs, slot_index), incoming)
        keep_here = pick(enc_keep, slot_index)
        result = lax.cond(
            active,
            lambda operand: encoder_forward(operand, enc_kernel, enc_gain, keep_here),
            lambda operand: operand,
            given,
        )
        enc_inputs = place(enc_inputs, given, slot_index, active)
        enc_outputs = place(enc_outputs, result, slot_index, active)
        passed = from_behind(result, "section", 1)
        arrived, wrap_slot = slot_of(step_index - last_level)
        bottom = place(bottom, passed, wrap_slot, arrived & (own_level == 0))
        return (passed, enc_inputs, enc_outputs, bottom)

    leftover, enc_inputs, enc_outputs, bottom = lax.fori_loop(
        0, loop_len, encoder_step, (blank, store_blank, store_blank, store_blank)
    )
    skip_acts = enc_outputs
    for bit_index in range(bit_count):
        skip_acts = swapped(skip_acts, "section", bit_index)
    dec_first = 0
    dec_source = bottom

    def decoder_step(step_index, loop_state):
        incoming, dec_inputs, dec_outputs = loop_state
        active, slot_index = slot_of(step_index - own_level)
        given = jnp.where(own_level == dec_first, pick(dec_source, slot_index), incoming)
        skip_here = pick(skip_acts, slot_index)
        keep_here = pick(dec_keep, slot_index)
        result = lax.cond(
            active,
            lambda operand: decoder_forward(operand, skip_here, dec_kernel, dec_gain, keep_here),
            lambda operand: operand,
            given,
        )
        dec_inputs = place(dec_inputs, given, slot_index, active)
        dec_outputs = place(dec_outputs, result, slot_index, active)
        passed = shifted(result, "section", 1)
        return (passed, dec_inputs, dec_outputs)

    leftover, dec_inputs, dec_outputs = lax.fori_loop(
        0, loop_len, decoder_step, (blank, store_blank, store_blank)
    )
    positions = noise_draw.shape[1] * noise_draw.shape[2] * noise_draw.shape[3]
    scale = 1.0 / math.sqrt(micro_count * lax.axis_size("dp") * positions)
    loss_grads = (
        (dec_outputs.astype(jnp.float32) - noise_draw.astype(jnp.float32)) * scale
    ).astype(jnp.bfloat16)
    gain_blank = jnp.zeros(enc_gain.shape, jnp.float32)
    back_order = last_level - own_level

    def decoder_back_step(step_index, loop_state):
        incoming, skip_grads, bottom_grads, act_store, gated_store, gain_acc = loop_state
        active, slot_index = slot_of(step_index - back_order)
        given = jnp.where(own_level == last_level, pick(loss_grads, slot_index), incoming)
        keep_here = pick(dec_keep, slot_index)

        def decoder_run(operand):
            stream_grad, skip_grad, activation, gated, gain_grad = decoder_backward(
                pick(dec_inputs, slot_index),
                pick(skip_acts, slot_index),
                operand,
                dec_kernel,
                dec_gain,
                keep_here,
            )
            return (stream_grad, skip_grad, activation, gated, gain_acc + gain_grad)

        def decoder_rest(operand):
            return (operand, operand, operand, operand, gain_acc)

        stream_grad, skip_grad, activation, gated, gain_acc = lax.cond(
            active, decoder_run, decoder_rest, given
        )
        skip_grads = place(skip_grads, skip_grad, slot_index, active)
        act_store = place(act_store, activation, slot_index, active)
        gated_store = place(gated_store, gated, slot_index, active)
        passed = from_behind(stream_grad, "section", -1)
        arrived, wrap_slot = slot_of(step_index - last_level)
        bottom_grads = place(bottom_grads, passed, wrap_slot, arrived & (own_level == last_level))
        return (passed, skip_grads, bottom_grads, act_store, gated_store, gain_acc)

    leftover, skip_grads, bottom_grads, dec_acts, dec_gated, dec_gain_acc = lax.fori_loop(
        0,
        loop_len,
        decoder_back_step,
        (blank, store_blank, store_blank, store_blank, store_blank, gain_blank),
    )
    dec_weight_acc = weight_term(temporal_columns(dec_acts), dec_gated.reshape(-1, channels))
    skip_cots = skip_grads
    for bit_index in range(bit_count):
        skip_cots = swapped(skip_cots, "section", bit_index)

    def encoder_back_step(step_index, loop_state):
        incoming, act_store, gated_store, gain_acc = loop_state
        active, slot_index = slot_of(step_index - (last_level - own_level))
        given = jnp.where(own_level == last_level, pick(bottom_grads, slot_index), incoming)
        keep_here = pick(enc_keep, slot_index)

        def encoder_run(operand):
            summed_grad = (
                operand.astype(jnp.float32) + pick(skip_cots, slot_index).astype(jnp.float32)
            ).astype(jnp.bfloat16)
            stream_grad, activation, gated, gain_grad = encoder_backward(
                pick(enc_inputs, slot_index), summed_grad, enc_kernel, enc_gain, keep_here
            )
            return (stream_grad, activation, gated, gain_acc + gain_grad)

        def encoder_rest(operand):
            return (operand, operand, operand, gain_acc)

        stream_grad, activation, gated, gain_acc = lax.cond(
            active, encoder_run, encoder_rest, given
        )
        act_store = place(act_store, activation, slot_index, active)
        gated_store = place(gated_store, gated, slot_index, active)
        passed = shifted(stream_grad, "section", -1)
        return (passed, act_store, gated_store, gain_acc)

    leftover, enc_acts, enc_gated, enc_gain_acc = lax.fori_loop(
        0, loop_len, encoder_back_step, (blank, store_blank, store_blank, gain_blank)
    )
    enc_weight_acc = weight_term(spatial_columns(enc_acts), enc_gated.reshape(-1, channels))
    enc_weight_out, enc_gain_out, dec_weight_out, dec_gain_out = (
        lax.psum_scatter(
            enc_weight_acc.astype(jnp.bfloat16), "dp", scatter_dimension=0, tiled=True
        ).astype(jnp.float32),
        lax.psum_scatter(
            enc_gain_acc.astype(jnp.bfloat16), "dp", scatter_dimension=1, tiled=True
        ).astype(jnp.float32),
        lax.psum_scatter(
            dec_weight_acc.astype(jnp.bfloat16), "dp", scatter_dimension=0, tiled=True
        ).astype(jnp.float32),
        lax.psum_scatter(
            dec_gain_acc.astype(jnp.bfloat16), "dp", scatter_dimension=1, tiled=True
        ).astype(jnp.float32),
    )
    return (enc_weight_out[None], enc_gain_out, dec_weight_out[None], dec_gain_out)


def solution(mesh):
    placed = (
        P("dp", None, None, None, None),
        P("dp"),
        P("dp"),
        P("dp", None, None, None, None),
        P("dp", None),
        P("section", None, None),
        P("section", None),
        P("section", None, None),
        P("section", None),
    )
    return jax.shard_map(
        body,
        mesh=mesh,
        in_specs=placed,
        out_specs=(
            P("section", "dp", None),
            P("section", "dp"),
            P("section", "dp", None),
            P("section", "dp"),
        ),
        check_vma=False,
    )
```

profile of v0, /device:TPU:0, one launch (start us, length us, event | category | flops | bytes accessed | tf_op | source)
XLA Modules:
  0.0 1023.9 jit_solution(10946919200995801433)
XLA Ops:
  13.7 194.4 %while.85 = (s32[]{:T(128)}, bf16[1,3,4,2,640]{4,2,3,1,0:T(4,128)(2,1)S(1)}, bf16[8,3,4,2,640]{4,2,3,1,0:T(4,128)(2,1)S(1)}, bf16[8,3,4,2,640]{4,2,3,1,0:T(4,128...) while((s32[]{:T(128)}, ...), condition=%wide.region_7.8_spmd, body=%wide.region_0.7_spmd.sunk | while | flops 177438752 | bytes 8974227 | solution.py:211
  138.5 9.9 collective-permute-done
  150.0 10.0 collective-permute-done
  161.7 9.9 collective-permute-done
  173.2 9.9 collective-permute-done
  184.7 10.2 collective-permute-done
  196.6 11.5 %collective-permute-done = bf16[1,3,4,2,640]{4,2,3,1,0:T(4,128)(2,1)S(1)} collective-permute-done((bf16[1,3,4,2,640]{4,2,3,1,0:T(4,128)(2,1)S(1)}, bf16[1,3,4,2,640]{4,2,3,1,0:T(4,128)(2,1)S(1)}, u32[]{:S(2)}, u32[]{:S(2)}) %collective-permute-start) | collective-permute-done | bytes 30752 | tf_op jit(solution)/shard_map/while/body/eval_jaxpr/ppermute | solution.py:13
  220.8 9.2 collective-permute-done.6
  230.9 141.0 %while.86 = (s32[]{:T(128)}, bf16[1,3,4,2,640]{4,2,3,1,0:T(4,128)(2,1)S(1)}, bf16[8,3,4,2,640]{4,2,3,1,0:T(4,128)(2,1)}, bf16[8,3,4,2,640]{4,3,2,1,0:T(2,128)(2,...) while((s32[]{:T(128)}, ...), condition=%wide.region_15.16_spmd, body=%wide.region_8.15_spmd.sunk | while | flops 59689000 | bytes 3463517 | solution.py:237
  377.0 254.1 %while.87 = (s32[]{:T(128)}, bf16[1,3,4,2,640]{4,2,3,1,0:T(4,128)(2,1)S(1)}, bf16[8,3,4,2,640]{4,2,3,1,0:T(4,128)(2,1)}, bf16[8,3,4,2,640]{4,2,3,1,0:T(4,128)(2,...) while((s32[]{:T(128)}, ...), condition=%wide.region_28.29_spmd, body=%wide.region_16.28_spmd.sunk | while | flops 59858156 | bytes 4660401 | solution.py:279
  378.5 18.5 %collective-permute-start.2 = (bf16[1,3,4,2,640]{4,2,3,1,0:T(4,128)(2,1)S(1)}, bf16[1,3,4,2,640]{4,2,3,1,0:T(4,128)(2,1)S(1)}, u32[]{:S(2)}, u32[]{:S(2)}) collective-permute-start(bf16[1,3,4,2,640]{4,2,3,1,0:T(4,128)(2,1)S(1)} %get-tuple-element.1832), channel_id=1, source_target_pairs={{0,28},{4,0},{8,4},{12,8},{16,12},{20,16},{24,20},{28,24},{1,29},{... | collective-permute-start | bytes 92168 | tf_op jit(solution)/shard_map/while/body/eval_jaxpr/ppermute | solution.py:13
  402.7 11.8 %collective-permute-start.2 = (bf16[1,3,4,2,640]{4,2,3,1,0:T(4,128)(2,1)S(1)}, bf16[1,3,4,2,640]{4,2,3,1,0:T(4,128)(2,1)S(1)}, u32[]{:S(2)}, u32[]{:S(2)}) collective-permute-start(bf16[1,3,4,2,640]{4,2,3,1,0:T(4,128)(2,1)S(1)} %get-tuple-element.1832), channel_id=1, source_target_pairs={{0,28},{4,0},{8,4},{12,8},{16,12},{20,16},{24,20},{28,24},{1,29},{... | collective-permute-start | bytes 92168 | tf_op jit(solution)/shard_map/while/body/eval_jaxpr/ppermute | solution.py:13
  420.2 11.8 %collective-permute-start.2 = (bf16[1,3,4,2,640]{4,2,3,1,0:T(4,128)(2,1)S(1)}, bf16[1,3,4,2,640]{4,2,3,1,0:T(4,128)(2,1)S(1)}, u32[]{:S(2)}, u32[]{:S(2)}) collective-permute-start(bf16[1,3,4,2,640]{4,2,3,1,0:T(4,128)(2,1)S(1)} %get-tuple-element.1832), channel_id=1, source_target_pairs={{0,28},{4,0},{8,4},{12,8},{16,12},{20,16},{24,20},{28,24},{1,29},{... | collective-permute-start | bytes 92168 | tf_op jit(solution)/shard_map/while/body/eval_jaxpr/ppermute | solution.py:13
  437.6 11.8 %collective-permute-start.2 = (bf16[1,3,4,2,640]{4,2,3,1,0:T(4,128)(2,1)S(1)}, bf16[1,3,4,2,640]{4,2,3,1,0:T(4,128)(2,1)S(1)}, u32[]{:S(2)}, u32[]{:S(2)}) collective-permute-start(bf16[1,3,4,2,640]{4,2,3,1,0:T(4,128)(2,1)S(1)} %get-tuple-element.1832), channel_id=1, source_target_pairs={{0,28},{4,0},{8,4},{12,8},{16,12},{20,16},{24,20},{28,24},{1,29},{... | collective-permute-start | bytes 92168 | tf_op jit(solution)/shard_map/while/body/eval_jaxpr/ppermute | solution.py:13
  455.1 11.8 %collective-permute-start.2 = (bf16[1,3,4,2,640]{4,2,3,1,0:T(4,128)(2,1)S(1)}, bf16[1,3,4,2,640]{4,2,3,1,0:T(4,128)(2,1)S(1)}, u32[]{:S(2)}, u32[]{:S(2)}) collective-permute-start(bf16[1,3,4,2,640]{4,2,3,1,0:T(4,128)(2,1)S(1)} %get-tuple-element.1832), channel_id=1, source_target_pairs={{0,28},{4,0},{8,4},{12,8},{16,12},{20,16},{24,20},{28,24},{1,29},{... | collective-permute-start | bytes 92168 | tf_op jit(solution)/shard_map/while/body/eval_jaxpr/ppermute | solution.py:13
  472.5 11.8 %collective-permute-start.2 = (bf16[1,3,4,2,640]{4,2,3,1,0:T(4,128)(2,1)S(1)}, bf16[1,3,4,2,640]{4,2,3,1,0:T(4,128)(2,1)S(1)}, u32[]{:S(2)}, u32[]{:S(2)}) collective-permute-start(bf16[1,3,4,2,640]{4,2,3,1,0:T(4,128)(2,1)S(1)} %get-tuple-element.1832), channel_id=1, source_target_pairs={{0,28},{4,0},{8,4},{12,8},{16,12},{20,16},{24,20},{28,24},{1,29},{... | collective-permute-start | bytes 92168 | tf_op jit(solution)/shard_map/while/body/eval_jaxpr/ppermute | solution.py:13
  490.0 11.8 %collective-permute-start.2 = (bf16[1,3,4,2,640]{4,2,3,1,0:T(4,128)(2,1)S(1)}, bf16[1,3,4,2,640]{4,2,3,1,0:T(4,128)(2,1)S(1)}, u32[]{:S(2)}, u32[]{:S(2)}) collective-permute-start(bf16[1,3,4,2,640]{4,2,3,1,0:T(4,128)(2,1)S(1)} %get-tuple-element.1832), channel_id=1, source_target_pairs={{0,28},{4,0},{8,4},{12,8},{16,12},{20,16},{24,20},{28,24},{1,29},{... | collective-permute-start | bytes 92168 | tf_op jit(solution)/shard_map/while/body/eval_jaxpr/ppermute | solution.py:13
  653.1 237.0 %while.88 = (s32[]{:T(128)}, bf16[1,3,4,2,640]{4,2,3,1,0:T(4,128)(2,1)S(1)}, bf16[8,3,4,2,640]{4,2,3,1,0:T(4,128)(2,1)S(1)}, bf16[8,3,4,2,640]{4,2,3,1,0:T(4,128...) while((s32[]{:T(128)}, ...), condition=%wide.region_41.42_spmd, body=%wide.region_29.41_spmd.sunk | while | flops 178053344 | bytes 10936407 | solution.py:316
  702.9 54.5 %collective-permute-done.3 = bf16[1,3,4,2,640]{4,2,3,1,0:T(4,128)(2,1)S(1)} collective-permute-done((bf16[1,3,4,2,640]{4,2,3,1,0:T(4,128)(2,1)S(1)}, bf16[1,3,4,2,640]{4,2,3,1,0:T(4,128)(2,1)S(1)}, u32[]{:S(2)}, u32[]{:S(2)}) %collective-permute-start.3) | collective-permute-done | bytes 30752 | tf_op jit(solution)/shard_map/while/body/eval_jaxpr/ppermute | solution.py:25
  758.2 9.2 conditional.11
  808.1 9.2 conditional.11
  841.9 9.2 conditional.11
  910.2 35.4 %reduce-scatter.11.cloned.1.call-done = bf16[480,640]{1,0:T(8,128)(2,1)} async-done(((bf16[1920,640]{1,0:T(8,128)(2,1)}), bf16[480,640]{1,0:T(8,128)(2,1)}) %reduce-scatter.11.cloned.1.call-update) | async-done | bytes 614416 | tf_op jit(solution)/shard_map/reduce_scatter | solution.py:327
  947.7 66.1 %reduce-scatter.9.cloned.1.call-done = bf16[1440,640]{1,0:T(8,128)(2,1)} async-done(((bf16[5760,640]{1,0:T(8,128)(2,1)}), bf16[1440,640]{1,0:T(8,128)(2,1)}) %reduce-scatter.9.cloned.1.call-update) | async-done | bytes 1843216 | tf_op jit(solution)/shard_map/reduce_scatter | solution.py:321
  (1330 shorter events, 893.3 us)
Async XLA Ops:
  7.2 893.4 %reduce-scatter.15.cloned.1.call-start = ((), (), s32[]{:S(2)}) async-start(), calls=%async_computation.7 | async-start | bytes 204800
  127.8 9.1 collective-permute-start
  137.0 11.4 %collective-permute-start = (bf16[1,3,4,2,640]{4,2,3,1,0:T(4,128)(2,1)S(1)}, bf16[1,3,4,2,640]{4,2,3,1,0:T(4,128)(2,1)S(1)}, u32[]{:S(2)}, u32[]{:S(2)}) collective-permute-start(bf16[1,3,4,2,640]{4,2,3,1,0:T(4,128)(2,1)S(1)} %get-tuple-element.2080), channel_id=1, source_target_pairs={{0,4},{4,8},{8,12},{12,16},{16,20},{20,24},{24,28},{28,0},{1,5},{5... | collective-permute-start | bytes 92168 | tf_op jit(solution)/shard_map/while/body/eval_jaxpr/ppermute | solution.py:13
  148.5 11.5 %collective-permute-start = (bf16[1,3,4,2,640]{4,2,3,1,0:T(4,128)(2,1)S(1)}, bf16[1,3,4,2,640]{4,2,3,1,0:T(4,128)(2,1)S(1)}, u32[]{:S(2)}, u32[]{:S(2)}) collective-permute-start(bf16[1,3,4,2,640]{4,2,3,1,0:T(4,128)(2,1)S(1)} %get-tuple-element.2080), channel_id=1, source_target_pairs={{0,4},{4,8},{8,12},{12,16},{16,20},{20,24},{24,28},{28,0},{1,5},{5... | collective-permute-start | bytes 92168 | tf_op jit(solution)/shard_map/while/body/eval_jaxpr/ppermute | solution.py:13
  160.2 11.4 %collective-permute-start = (bf16[1,3,4,2,640]{4,2,3,1,0:T(4,128)(2,1)S(1)}, bf16[1,3,4,2,640]{4,2,3,1,0:T(4,128)(2,1)S(1)}, u32[]{:S(2)}, u32[]{:S(2)}) collective-permute-start(bf16[1,3,4,2,640]{4,2,3,1,0:T(4,128)(2,1)S(1)} %get-tuple-element.2080), channel_id=1, source_target_pairs={{0,4},{4,8},{8,12},{12,16},{16,20},{20,24},{24,28},{28,0},{1,5},{5... | collective-permute-start | bytes 92168 | tf_op jit(solution)/shard_map/while/body/eval_jaxpr/ppermute | solution.py:13
  171.7 11.4 %collective-permute-start = (bf16[1,3,4,2,640]{4,2,3,1,0:T(4,128)(2,1)S(1)}, bf16[1,3,4,2,640]{4,2,3,1,0:T(4,128)(2,1)S(1)}, u32[]{:S(2)}, u32[]{:S(2)}) collective-permute-start(bf16[1,3,4,2,640]{4,2,3,1,0:T(4,128)(2,1)S(1)} %get-tuple-element.2080), channel_id=1, source_target_pairs={{0,4},{4,8},{8,12},{12,16},{16,20},{20,24},{24,28},{28,0},{1,5},{5... | collective-permute-start | bytes 92168 | tf_op jit(solution)/shard_map/while/body/eval_jaxpr/ppermute | solution.py:13
  183.3 11.7 %collective-permute-start = (bf16[1,3,4,2,640]{4,2,3,1,0:T(4,128)(2,1)S(1)}, bf16[1,3,4,2,640]{4,2,3,1,0:T(4,128)(2,1)S(1)}, u32[]{:S(2)}, u32[]{:S(2)}) collective-permute-start(bf16[1,3,4,2,640]{4,2,3,1,0:T(4,128)(2,1)S(1)} %get-tuple-element.2080), channel_id=1, source_target_pairs={{0,4},{4,8},{8,12},{12,16},{16,20},{20,24},{24,28},{28,0},{1,5},{5... | collective-permute-start | bytes 92168 | tf_op jit(solution)/shard_map/while/body/eval_jaxpr/ppermute | solution.py:13
  195.1 13.0 %collective-permute-start = (bf16[1,3,4,2,640]{4,2,3,1,0:T(4,128)(2,1)S(1)}, bf16[1,3,4,2,640]{4,2,3,1,0:T(4,128)(2,1)S(1)}, u32[]{:S(2)}, u32[]{:S(2)}) collective-permute-start(bf16[1,3,4,2,640]{4,2,3,1,0:T(4,128)(2,1)S(1)} %get-tuple-element.2080), channel_id=1, source_target_pairs={{0,4},{4,8},{8,12},{12,16},{16,20},{20,24},{24,28},{28,0},{1,5},{5... | collective-permute-start | bytes 92168 | tf_op jit(solution)/shard_map/while/body/eval_jaxpr/ppermute | solution.py:13
  220.8 9.2 collective-permute-start.6
  311.2 9.4 collective-permute-start.1
  330.1 9.4 collective-permute-start.1
  378.5 21.3 %collective-permute-start.2 = (bf16[1,3,4,2,640]{4,2,3,1,0:T(4,128)(2,1)S(1)}, bf16[1,3,4,2,640]{4,2,3,1,0:T(4,128)(2,1)S(1)}, u32[]{:S(2)}, u32[]{:S(2)}) collective-permute-start(bf16[1,3,4,2,640]{4,2,3,1,0:T(4,128)(2,1)S(1)} %get-tuple-element.1832), channel_id=1, source_target_pairs={{0,28},{4,0},{8,4},{12,8},{16,12},{20,16},{24,20},{28,24},{1,29},{... | collective-permute-start | bytes 92168 | tf_op jit(solution)/shard_map/while/body/eval_jaxpr/ppermute | solution.py:13
  402.7 14.6 %collective-permute-start.2 = (bf16[1,3,4,2,640]{4,2,3,1,0:T(4,128)(2,1)S(1)}, bf16[1,3,4,2,640]{4,2,3,1,0:T(4,128)(2,1)S(1)}, u32[]{:S(2)}, u32[]{:S(2)}) collective-permute-start(bf16[1,3,4,2,640]{4,2,3,1,0:T(4,128)(2,1)S(1)} %get-tuple-element.1832), channel_id=1, source_target_pairs={{0,28},{4,0},{8,4},{12,8},{16,12},{20,16},{24,20},{28,24},{1,29},{... | collective-permute-start | bytes 92168 | tf_op jit(solution)/shard_map/while/body/eval_jaxpr/ppermute | solution.py:13
  420.2 14.6 %collective-permute-start.2 = (bf16[1,3,4,2,640]{4,2,3,1,0:T(4,128)(2,1)S(1)}, bf16[1,3,4,2,640]{4,2,3,1,0:T(4,128)(2,1)S(1)}, u32[]{:S(2)}, u32[]{:S(2)}) collective-permute-start(bf16[1,3,4,2,640]{4,2,3,1,0:T(4,128)(2,1)S(1)} %get-tuple-element.1832), channel_id=1, source_target_pairs={{0,28},{4,0},{8,4},{12,8},{16,12},{20,16},{24,20},{28,24},{1,29},{... | collective-permute-start | bytes 92168 | tf_op jit(solution)/shard_map/while/body/eval_jaxpr/ppermute | solution.py:13
  437.6 14.6 %collective-permute-start.2 = (bf16[1,3,4,2,640]{4,2,3,1,0:T(4,128)(2,1)S(1)}, bf16[1,3,4,2,640]{4,2,3,1,0:T(4,128)(2,1)S(1)}, u32[]{:S(2)}, u32[]{:S(2)}) collective-permute-start(bf16[1,3,4,2,640]{4,2,3,1,0:T(4,128)(2,1)S(1)} %get-tuple-element.1832), channel_id=1, source_target_pairs={{0,28},{4,0},{8,4},{12,8},{16,12},{20,16},{24,20},{28,24},{1,29},{... | collective-permute-start | bytes 92168 | tf_op jit(solution)/shard_map/while/body/eval_jaxpr/ppermute | solution.py:13
  455.1 14.6 %collective-permute-start.2 = (bf16[1,3,4,2,640]{4,2,3,1,0:T(4,128)(2,1)S(1)}, bf16[1,3,4,2,640]{4,2,3,1,0:T(4,128)(2,1)S(1)}, u32[]{:S(2)}, u32[]{:S(2)}) collective-permute-start(bf16[1,3,4,2,640]{4,2,3,1,0:T(4,128)(2,1)S(1)} %get-tuple-element.1832), channel_id=1, source_target_pairs={{0,28},{4,0},{8,4},{12,8},{16,12},{20,16},{24,20},{28,24},{1,29},{... | collective-permute-start | bytes 92168 | tf_op jit(solution)/shard_map/while/body/eval_jaxpr/ppermute | solution.py:13
  472.5 14.6 %collective-permute-start.2 = (bf16[1,3,4,2,640]{4,2,3,1,0:T(4,128)(2,1)S(1)}, bf16[1,3,4,2,640]{4,2,3,1,0:T(4,128)(2,1)S(1)}, u32[]{:S(2)}, u32[]{:S(2)}) collective-permute-start(bf16[1,3,4,2,640]{4,2,3,1,0:T(4,128)(2,1)S(1)} %get-tuple-element.1832), channel_id=1, source_target_pairs={{0,28},{4,0},{8,4},{12,8},{16,12},{20,16},{24,20},{28,24},{1,29},{... | collective-permute-start | bytes 92168 | tf_op jit(solution)/shard_map/while/body/eval_jaxpr/ppermute | solution.py:13
  490.0 14.6 %collective-permute-start.2 = (bf16[1,3,4,2,640]{4,2,3,1,0:T(4,128)(2,1)S(1)}, bf16[1,3,4,2,640]{4,2,3,1,0:T(4,128)(2,1)S(1)}, u32[]{:S(2)}, u32[]{:S(2)}) collective-permute-start(bf16[1,3,4,2,640]{4,2,3,1,0:T(4,128)(2,1)S(1)} %get-tuple-element.1832), channel_id=1, source_target_pairs={{0,28},{4,0},{8,4},{12,8},{16,12},{20,16},{24,20},{28,24},{1,29},{... | collective-permute-start | bytes 92168 | tf_op jit(solution)/shard_map/while/body/eval_jaxpr/ppermute | solution.py:13
  643.7 9.2 collective-permute-start.9
  645.6 263.1 %reduce-scatter.13.cloned.1.call-start = ((), (), s32[]{:S(2)}) async-start(), calls=%async_computation.6 | async-start | bytes 204800
  701.6 55.9 %collective-permute-start.3 = (bf16[1,3,4,2,640]{4,2,3,1,0:T(4,128)(2,1)S(1)}, bf16[1,3,4,2,640]{4,2,3,1,0:T(4,128)(2,1)S(1)}, u32[]{:S(2)}, u32[]{:S(2)}) collective-permute-start(bf16[1,3,4,2,640]{4,2,3,1,0:T(4,128)(2,1)S(1)} %get-tuple-element.1852), channel_id=1, source_target_pairs={{4,0},{8,4},{12,8},{16,12},{20,16},{24,20},{28,24},{5,1},{9,5},{13... | collective-permute-start | bytes 92168 | tf_op jit(solution)/shard_map/while/body/eval_jaxpr/ppermute | solution.py:25
  817.3 7.2 collective-permute-start.3
  890.9 54.6 %reduce-scatter.11.cloned.1.call-start = ((), (), s32[]{:S(2)}) async-start(), calls=%async_computation.5 | async-start | bytes 3072000 | tf_op jit(solution)/shard_map/reduce_scatter | solution.py:327
  894.6 119.2 %reduce-scatter.9.cloned.1.call-start = ((), (), s32[]{:S(2)}) async-start(), calls=%async_computation.4 | async-start | bytes 9216000 | tf_op jit(solution)/shard_map/reduce_scatter | solution.py:321
  (52 other events, 1238.3 us)
Sparse Core Ops, SparseCore 0:
  645.7 20.7 reduce-scatter.14
  891.1 17.5 reduce-scatter.12
  911.8 33.6 reduce-scatter.10
  948.1 65.6 reduce-scatter.8
where the time goes:
time: 1040 us; the launch traced here: 1020 us
  waiting for transfers between devices  408 us (39%)
  other arithmetic  209 us (20%)
  starting transfers between devices  194 us (19%)
  matrix products  111 us (11%)
  local copies, waits for them, and re-layouts  81.4 us (8%)
  between operations  14.1 us (1%)
    ppermute x30, waiting for transfers between devices, shifted(): lax.ppermute(value, axis, [(source, source + steps) for source in range(f...  142 us
    ppermute x30, waiting for transfers between devices, from_behind(): lax.ppermute(value, axis, [(i, (i + by) % length) for i in range(length)])  117 us
    select_n x135, other arithmetic, place(): jnp.where(active, lax.dynamic_update_slice_in_dim(stack, piece, index, 0)...  114 us
    ppermute x30, starting transfers between devices, from_behind(): lax.ppermute(value, axis, [(i, (i + by) % length) for i in range(length)])  98.9 us
    ppermute x30, starting transfers between devices, shifted(): lax.ppermute(value, axis, [(source, source + steps) for source in range(f...  93.7 us
    reduce_scatter x1, waiting for transfers between devices, body(): lax.psum_scatter(enc_weight_acc.astype(jnp.bfloat16), 'dp', scatter_dimen...  66.1 us
    dot_general x8, matrix products, encoder_backward(): lax.dot_general(gated.reshape(-1, stream.shape[-1]), weight, (((1,), (1,)...  41.9 us
    ppermute x6, waiting for transfers between devices, swapped(): return lax.ppermute(value, axis, pairs)  39.9 us
  transfers between devices with their start and end apart: 70, of which 61 were waited for; matrix products, arithmetic and copies ran while one was open for 17% of the time, Pallas kernels for 0%

commit v1 on v0

v1 whole, which is shorter than its diff:
```python
import functools
import math

import jax
import jax.numpy as jnp
import numpy as np
from jax import lax
from jax.experimental import pallas as pl
from jax.experimental.pallas import tpu as pltpu
from jax.sharding import PartitionSpec as P

GROUPS = 32
ENC_TAPS = 9
DEC_TAPS = 3
KERNELS_OF_A_CHAIN = 32
BF16 = jnp.bfloat16
F32 = jnp.float32
VMEM_LIMIT = 32 * 1024 * 1024


def noise_level(timesteps):
    phase_arg = (timesteps.astype(F32) / 1000.0 + 0.008) / 1.008
    return jnp.cos(phase_arg * (math.pi / 2.0)) ** 2


def group_means(sums, spread_matrix, count, splits):
    rest = sums
    pieces = []
    for _ in range(splits - 1):
        piece = rest.astype(BF16).astype(F32)
        pieces.append(piece)
        rest = rest - piece
    pieces.append(rest)
    number = sums.shape[0]
    parts = jnp.concatenate(pieces, axis=0).astype(BF16)
    spread = jnp.dot(parts, spread_matrix, preferred_element_type=F32)
    total = spread[:number]
    for place in range(1, splits):
        total = total + spread[place * number : (place + 1) * number]
    folded = total.reshape(number // 8, 8, sums.shape[1])
    return jnp.sum(folded, axis=1, keepdims=True) * (1.0 / count)


def eight_rows(values):
    return jnp.sum(values.reshape(-1, 8, values.shape[-1]), axis=0)


def sigmoid(z):
    return 0.5 * jnp.tanh(0.5 * z) + 0.5


def spatial_shift(frames, row_offset, col_offset, height, width):
    step = row_offset * width + col_offset
    length = height * width
    moved = pltpu.roll(frames, (-step) % length, axis=1) if step % length else frames
    if row_offset == 0 and col_offset == 0:
        return moved
    place = lax.broadcasted_iota(jnp.int32, (1, length, 1), 1)
    row = place // width + row_offset
    col = place % width + col_offset
    inside = (row >= 0) & (row < height) & (col >= 0) & (col < width)
    return jnp.where(inside, moved, 0.0)


def spatial_columns_into(cols_ref, values_ref, sizes, sign):
    each = sizes.height * sizes.width
    pair = 2 * each
    channels = sizes.channels

    def one_pair(index, carry):
        place = pl.ds(pl.multiple_of(index * pair, pair), pair)
        frames = values_ref[place].reshape(2, each, channels)
        for tap in range(ENC_TAPS):
            moved = spatial_shift(
                frames, sign * (tap // 3 - 1), sign * (tap % 3 - 1), sizes.height, sizes.width
            )
            cols_ref[tap // 3, place, (tap % 3) * channels : (tap % 3 + 1) * channels] = (
                moved.reshape(pair, channels).astype(BF16)
            )
        return carry

    lax.fori_loop(0, sizes.rows // pair, one_pair, 0)


def temporal_pieces(values, frames, sign):
    samples, length, channels = values.shape
    each = length // frames
    blank = jnp.zeros((samples, each, channels), F32)
    before = jnp.concatenate([blank, values[:, : length - each]], axis=1)
    after = jnp.concatenate([values[:, each:], blank], axis=1)
    ordered = (before, values, after) if sign > 0 else (after, values, before)
    return [piece.reshape(samples * length, channels).astype(BF16) for piece in ordered]


def dot_nt(left, right):
    return lax.dot_general(left, right, (((1,), (1,)), ((), ())), preferred_element_type=F32)


class Sizes:
    def __init__(self, noise_draw, sections):
        self.micro, self.frames, self.height, self.width, self.channels = noise_draw.shape
        self.length = self.frames * self.height * self.width
        self.per_step = max(1, self.micro * sections // KERNELS_OF_A_CHAIN)
        self.steps = self.micro // self.per_step
        self.rows = self.per_step * self.length
        self.count = self.length * (self.channels // GROUPS)
        self.total = self.micro * self.length

    def sample(self, index):
        return slice(index * self.length, (index + 1) * self.length)


def norm_forward(sizes, step, values_ref, gain, spread_matrix, xhat_ref, rstd_ref):
    samples = range(sizes.per_step)
    sums = jnp.concatenate([eight_rows(values_ref[sizes.sample(s)]) for s in samples], axis=0)
    mean = group_means(sums, spread_matrix, sizes.count, 3)
    squares = []
    for s in samples:
        center = values_ref[sizes.sample(s)] - mean[s]
        values_ref[sizes.sample(s)] = center
        squares.append(eight_rows(center * center))
    spread = group_means(jnp.concatenate(squares, axis=0), spread_matrix, sizes.count, 3)
    rstd = lax.rsqrt(spread + 1e-05)
    for s in samples:
        first = step * sizes.rows + s * sizes.length
        normed = values_ref[sizes.sample(s)] * rstd[s]
        xhat_ref[first : first + sizes.length] = normed
        rstd_ref[step * sizes.per_step + s] = rstd[s]
        z = normed * gain
        values_ref[sizes.sample(s)] = z * sigmoid(z)


def residual(sizes, step, base_ref, keep_ref, branch_ref):
    out = []
    for s in range(sizes.per_step):
        index = step * sizes.per_step + s
        keep = keep_ref[index : index + 1]
        out.append(base_ref[sizes.sample(s)] + keep * branch_ref[sizes.sample(s)])
    return jnp.concatenate(out, axis=0)


def enc_forward_kernel(sizes, level, step, x_ref, w_ref, gain_ref, keep_ref, spread_ref, *refs):
    y_ref, xhat_ref, rstd_ref, act_ref, cols_ref, base_ref, values_ref, half_ref, sem = refs[-9:]

    @pl.when(lax.axis_index("section") == level)
    def _():
        x = x_ref[...].astype(F32)
        base_ref[...] = x
        values_ref[...] = x
        norm_forward(
            sizes, step, values_ref, gain_ref[...], spread_ref[...], xhat_ref, rstd_ref
        )
        half_ref[...] = values_ref[...].astype(BF16)
        part = pl.ds(step * sizes.rows, sizes.rows)
        store = pltpu.make_async_copy(half_ref, act_ref.at[part], sem)
        store.start()
        spatial_columns_into(cols_ref, values_ref, sizes, 1)

        def add_third(third, carry):
            part = jnp.dot(cols_ref[third], w_ref[third], preferred_element_type=F32)
            values_ref[...] = jnp.where(third == 0, part, values_ref[...] + part)
            return carry

        lax.fori_loop(0, 3, add_third, 0)
        y_ref[...] = residual(sizes, step, base_ref, keep_ref, values_ref).astype(BF16)
        store.wait()


def dec_forward_kernel(
    sizes, level, step, first, scale, x_ref, skip_ref, w_ref, gain_ref, keep_ref, spread_ref, *refs
):
    y_ref, xhat_ref, rstd_ref, act_ref, base_ref, values_ref, half_ref, sem = refs[-8:]

    @pl.when(lax.axis_index("section") == level)
    def _():
        x = x_ref[...].astype(F32)
        base_ref[...] = x
        values_ref[...] = x + (x if first else skip_ref[...].astype(F32))
        norm_forward(
            sizes, step, values_ref, gain_ref[...], spread_ref[...], xhat_ref, rstd_ref
        )
        half_ref[...] = values_ref[...].astype(BF16)
        part = pl.ds(step * sizes.rows, sizes.rows)
        store = pltpu.make_async_copy(half_ref, act_ref.at[part], sem)
        store.start()
        act = values_ref[...].reshape(sizes.per_step, sizes.length, sizes.channels)
        columns = jnp.concatenate(temporal_pieces(act, sizes.frames, 1), axis=1)
        values_ref[...] = jnp.dot(columns, w_ref[...], preferred_element_type=F32)
        out = residual(sizes, step, base_ref, keep_ref, values_ref).astype(BF16)
        if scale is not None:
            noise_ref = refs[0]
            out = ((out.astype(F32) - noise_ref[part].astype(F32)) * scale).astype(BF16)
        y_ref[...] = out
        store.wait()


def norm_back(sizes, step, cot_ref, gain, spread_matrix, xhat_ref, rstd_ref):
    samples = range(sizes.per_step)
    sums, products = [], []
    gain_rows = 0.0
    for s in samples:
        first = step * sizes.rows + s * sizes.length
        normed = xhat_ref[first : first + sizes.length]
        z = normed * gain
        sig = sigmoid(z)
        dz = cot_ref[sizes.sample(s)] * (sig * (1.0 + z * (1.0 - sig)))
        gain_rows = gain_rows + eight_rows(dz * normed)
        dn = dz * gain
        cot_ref[sizes.sample(s)] = dn
        sums.append(eight_rows(dn))
        products.append(eight_rows(dn * normed))
    means = group_means(jnp.concatenate(sums + products, axis=0), spread_matrix, sizes.count, 2)
    for s in samples:
        first = step * sizes.rows + s * sizes.length
        normed = xhat_ref[first : first + sizes.length]
        rstd = rstd_ref[step * sizes.per_step + s]
        cot_ref[sizes.sample(s)] = rstd * (
            cot_ref[sizes.sample(s)] - means[s] - normed * means[sizes.per_step + s]
        )
    return gain_rows


def add_gain(sizes, step, gain_acc_ref, gain_rows, cot_ref, half_ref, sem):
    total = gain_rows if step == 0 else gain_acc_ref[...] + gain_rows
    gain_acc_ref[...] = total
    if step == sizes.steps - 1:
        row = jnp.sum(total, axis=0, keepdims=True)
        tail = jnp.concatenate([row, jnp.zeros((15, sizes.channels), F32)], axis=0)
        half_ref[:16] = tail.astype(BF16)
        copy = pltpu.make_async_copy(
            half_ref.at[pl.ds(0, 16)], cot_ref.at[pl.ds(sizes.total, 16)], sem
        )
        copy.start()
        copy.wait()


def gate(sizes, step, keep_ref, values):
    out = []
    for s in range(sizes.per_step):
        index = step * sizes.per_step + s
        out.append(keep_ref[index : index + 1] * values[sizes.sample(s)])
    return jnp.concatenate(out, axis=0)


def enc_backward_kernel(
    sizes, level, step, last, x_ref, skip_ref, w_ref, gain_ref, keep_ref, spread_ref, xhat_ref, rstd_ref, *refs
):
    y_ref, gain_acc_ref, cot_ref, cols_ref, base_ref, values_ref, half_ref, sem = refs[-8:]

    @pl.when(lax.axis_index("section") == level)
    def _():
        t = x_ref[...]
        if not last:
            t = (t.astype(F32) + skip_ref[...].astype(F32)).astype(BF16)
        t = t.astype(F32)
        base_ref[...] = t
        gated = gate(sizes, step, keep_ref, t)
        values_ref[...] = gated
        half_ref[...] = gated.astype(BF16)
        part = pl.ds(step * sizes.rows, sizes.rows)
        store = pltpu.make_async_copy(half_ref, cot_ref.at[part], sem)
        store.start()
        spatial_columns_into(cols_ref, values_ref, sizes, -1)

        def add_third(third, carry):
            part = jnp.zeros((sizes.rows, sizes.channels), F32)
            for tap in range(3):
                where = slice(tap * sizes.channels, (tap + 1) * sizes.channels)
                part = part + dot_nt(cols_ref[third, :, where], w_ref[third, where, :])
            values_ref[...] = jnp.where(third == 0, part, values_ref[...] + part)
            return carry

        lax.fori_loop(0, 3, add_third, 0)
        gain_rows = norm_back(
            sizes, step, values_ref, gain_ref[...], spread_ref[...], xhat_ref, rstd_ref
        )
        y_ref[...] = (base_ref[...] + values_ref[...]).astype(BF16)
        store.wait()
        add_gain(sizes, step, gain_acc_ref, gain_rows, cot_ref, half_ref, sem)


def dec_backward_kernel(
    sizes, level, step, first, x_ref, w_ref, gain_ref, keep_ref, spread_ref, xhat_ref, rstd_ref, *refs
):
    y_ref = refs[-8 if not first else -7]
    skip_cot_ref = refs[-7]
    gain_acc_ref, cot_ref, base_ref, values_ref, half_ref, sem = refs[-6:]

    @pl.when(lax.axis_index("section") == level)
    def _():
        g = x_ref[...].astype(F32)
        base_ref[...] = g
        gated = gate(sizes, step, keep_ref, g)
        half_ref[...] = gated.astype(BF16)
        part = pl.ds(step * sizes.rows, sizes.rows)
        store = pltpu.make_async_copy(half_ref, cot_ref.at[part], sem)
        store.start()
        pieces = temporal_pieces(
            gated.reshape(sizes.per_step, sizes.length, sizes.channels), sizes.frames, -1
        )
        back = jnp.zeros((sizes.rows, sizes.channels), F32)
        for tap in range(DEC_TAPS):
            where = slice(tap * sizes.channels, (tap + 1) * sizes.channels)
            back = back + dot_nt(pieces[tap], w_ref[where, :])
        values_ref[...] = back
        gain_rows = norm_back(
            sizes, step, values_ref, gain_ref[...], spread_ref[...], xhat_ref, rstd_ref
        )
        grad = values_ref[...]
        out = (base_ref[...] + grad).astype(BF16)
        skip_cot = grad.astype(BF16)
        if first:
            out = (out.astype(F32) + skip_cot.astype(F32)).astype(BF16)
        else:
            skip_cot_ref[...] = skip_cot
        y_ref[...] = out
        store.wait()
        add_gain(sizes, step, gain_acc_ref, gain_rows, cot_ref, half_ref, sem)


def tap_span(rows_out, channels, taps, parts):
    span = 0
    for index in range(parts):
        start = index * rows_out
        span = max(span, -(-(start % channels + rows_out) // channels))
    return min(span, taps)


def weight_kernel(sizes, taps, span, rows_out, act_ref, cot_ref, out_ref, gain_out_ref, wide_ref):
    me = lax.axis_index("dp")
    groups = act_ref.shape[0]
    valid = sizes.micro * sizes.length
    rows = groups * valid
    base = jnp.minimum(me * rows_out // sizes.channels, taps - span)
    act = act_ref[...].reshape(rows, sizes.channels).astype(F32)
    cot = cot_ref[:, :valid, :].reshape(rows, sizes.channels)
    each = sizes.height * sizes.width
    gain_out_ref[...] = jnp.sum(cot_ref[:, valid : valid + 16, :].astype(F32), axis=0)[:8]
    for tap in range(taps):

        @pl.when((tap >= base) & (tap < base + span))
        def _(tap=tap):
            if taps == ENC_TAPS:
                frames = act.reshape(rows // each, each, sizes.channels)
                moved = spatial_shift(frames, tap // 3 - 1, tap % 3 - 1, sizes.height, sizes.width)
                moved = moved.reshape(rows, sizes.channels).astype(BF16)
            else:
                values = act.reshape(rows // sizes.length, sizes.length, sizes.channels)
                moved = temporal_pieces(values, sizes.frames, 1)[tap]
            place = pl.multiple_of((tap - base) * sizes.channels, sizes.channels)
            wide_ref[pl.ds(place, sizes.channels)] = lax.dot_general(
                moved, cot, (((0,), (0,)), ((), ())), preferred_element_type=F32
            )

    offset = pl.multiple_of(me * rows_out - base * sizes.channels, 16)
    out_ref[...] = wide_ref[pl.ds(offset, rows_out)]


def load_kernel(enc_ref, dec_ref, spread_ref, enc_out, dec_out, spread_out, sems):
    copies = [
        pltpu.make_async_copy(enc_ref, enc_out, sems.at[0]),
        pltpu.make_async_copy(dec_ref, dec_out, sems.at[1]),
        pltpu.make_async_copy(spread_ref, spread_out, sems.at[2]),
    ]
    for copy in copies:
        copy.start()
    for copy in copies:
        copy.wait()


VM = pl.BlockSpec(memory_space=pltpu.VMEM)
ANY = pl.BlockSpec(memory_space=pl.ANY)


def params():
    return pltpu.CompilerParams(vmem_limit_bytes=VMEM_LIMIT)


def in_vmem(value):
    return pltpu.with_memory_space_constraint(value, pltpu.VMEM)


def staged_call(kernel, inputs, plain_outs, kept, far, state, scratch, flops):
    number = len(inputs)
    inputs = [in_vmem(value) for value in inputs]
    in_specs = [VM] * number
    aliases = {}
    if state is not None:
        for place in range(len(state)):
            aliases[number + place] = len(plain_outs) + place
        inputs = inputs + [in_vmem(value) for value in state[: len(kept)]] + list(state[len(kept) :])
        in_specs = in_specs + [VM] * len(kept) + [ANY] * len(far)
    outs = pl.pallas_call(
        kernel,
        in_specs=in_specs,
        out_specs=[VM] * (len(plain_outs) + len(kept)) + [ANY] * len(far),
        out_shape=[pltpu.VMEM(s, d) for s, d in list(plain_outs) + list(kept)]
        + [jax.ShapeDtypeStruct(s, d) for s, d in far],
        scratch_shapes=scratch,
        input_output_aliases=aliases,
        compiler_params=params(),
        cost_estimate=pl.CostEstimate(flops=flops, bytes_accessed=0, transcendentals=0),
    )(*inputs)
    return outs[: len(plain_outs)], outs[len(plain_outs) :]


def body(
    clip_pool,
    sample_ids,
    timesteps,
    noise_draw,
    keep_lists,
    enc_weight,
    enc_gain,
    dec_weight,
    dec_gain,
):
    sections = lax.axis_size("section")
    parts = lax.axis_size("dp")
    own_level = lax.axis_index("section")
    sizes = Sizes(noise_draw, sections)
    channels, rows, steps = sizes.channels, sizes.rows, sizes.steps
    total_rows = sizes.total
    scale = 1.0 / math.sqrt(sizes.micro * parts * sizes.length)

    channel = np.arange(channels) // (channels // GROUPS)
    spread_matrix = jnp.asarray(channel[:, None] == channel[None, :], BF16)
    enc_taps = enc_weight.reshape(3, 3 * channels, channels)
    dec_taps = dec_weight.reshape(DEC_TAPS * channels, channels)
    enc_taps, dec_taps, spread_matrix = pl.pallas_call(
        load_kernel,
        in_specs=[ANY] * 3,
        out_specs=[VM] * 3,
        out_shape=[
            pltpu.VMEM(enc_taps.shape, BF16),
            pltpu.VMEM(dec_taps.shape, BF16),
            pltpu.VMEM(spread_matrix.shape, BF16),
        ],
        scratch_shapes=[pltpu.SemaphoreType.DMA((3,))],
        compiler_params=params(),
    )(enc_taps, dec_taps, spread_matrix)

    keep_rates = keep_lists.astype(F32)
    own_keep = [
        jnp.broadcast_to(
            lax.dynamic_slice_in_dim(keep_rates, own_level + shift, 1, 1), (sizes.micro, channels)
        )
        for shift in (0, sections)
    ]
    clean = jnp.take(clip_pool, sample_ids, axis=0).astype(F32)
    level_noise = noise_level(timesteps)[:, None, None, None, None]
    start = (
        jnp.sqrt(level_noise) * clean + jnp.sqrt(1.0 - level_noise) * noise_draw.astype(F32)
    ).astype(BF16)
    start = start.reshape(steps, rows, channels)
    noise_rows = noise_draw.reshape(total_rows, channels)

    row_shape = ((rows, channels), BF16)
    forward_state = (
        [((total_rows, channels), F32), ((sizes.micro, 1, channels), F32)],
        [((total_rows, channels), BF16)],
    )
    back_state = ([((8, channels), F32)], [((total_rows + 16, channels), BF16)])
    work = [
        pltpu.VMEM((rows, channels), F32),
        pltpu.VMEM((rows, channels), F32),
        pltpu.VMEM((rows, channels), BF16),
        pltpu.SemaphoreType.DMA,
    ]
    cols = [pltpu.VMEM((3, rows, 3 * channels), BF16)] + work
    enc_flops = 2 * rows * ENC_TAPS * channels * channels
    dec_flops = 2 * rows * DEC_TAPS * channels * channels

    def send(value, source, target):
        return lax.ppermute(value, "section", [(source, target)])

    last = sections - 1
    current = [start[step] for step in range(steps)]
    skips = [None] * sections
    enc_state = None
    for level in range(sections):
        sent = []
        skip = []
        for step in range(steps):
            (y,), enc_state = staged_call(
                functools.partial(enc_forward_kernel, sizes, level, step),
                [current[step], enc_taps, enc_gain, own_keep[0], spread_matrix],
                [row_shape],
                *forward_state,
                enc_state,
                cols,
                enc_flops,
            )
            sent.append(send(y, level, (level + 1) % sections))
            if level < last:
                skip.append(send(y, level, last - level))
        current = sent
        skips[level] = skip
    enc_xhat, enc_rstd, enc_act = enc_state
    enc_act_all = lax.all_gather(enc_act, "dp")

    dec_state = None
    for level in range(sections):
        sent = []
        for step in range(steps):
            first = level == 0
            skip = current[step] if first else skips[last - level][step]
            final = level == last
            extra = [noise_rows] if final else []
            kernel = functools.partial(
                dec_forward_kernel, sizes, level, step, first, scale if final else None
            )
            inputs = [current[step], skip, dec_taps, dec_gain, own_keep[1], spread_matrix] + extra
            (y,), dec_state = staged_call(
                kernel, inputs, [row_shape], *forward_state, dec_state, work, dec_flops
            )
            sent.append(y if final else send(y, level, level + 1))
        current = sent
    dec_xhat, dec_rstd, dec_act = dec_state
    dec_act_all = lax.all_gather(dec_act, "dp")

    skip_cots = [None] * sections
    state = None
    for level in reversed(range(sections)):
        sent = []
        cots = []
        first = level == 0
        for step in range(steps):
            outs, state = staged_call(
                functools.partial(dec_backward_kernel, sizes, level, step, first),
                [current[step], dec_taps, dec_gain, own_keep[1], spread_matrix, dec_xhat, dec_rstd],
                [row_shape] if first else [row_shape, row_shape],
                *back_state,
                state,
                work,
                dec_flops,
            )
            sent.append(send(outs[0], level, last if first else level - 1))
            if not first:
                cots.append(send(outs[1], level, last - level))
        current = sent
        skip_cots[last - level] = cots
    dec_cot_all = lax.all_gather(state[1], "dp")

    def weight_grad(act_all, cot_all, taps):
        rows_out = taps * channels // parts
        span = tap_span(rows_out, channels, taps, parts)
        grad, gain = pl.pallas_call(
            functools.partial(weight_kernel, sizes, taps, span, rows_out),
            in_specs=[VM, VM],
            out_specs=[VM, VM],
            out_shape=[
                jax.ShapeDtypeStruct((rows_out, channels), F32),
                jax.ShapeDtypeStruct((8, channels), F32),
            ],
            scratch_shapes=[pltpu.VMEM((span * channels, channels), F32)],
            compiler_params=params(),
            cost_estimate=pl.CostEstimate(
                flops=2 * span * channels * channels * parts * total_rows,
                bytes_accessed=rows_out * channels * 4,
                transcendentals=0,
            ),
        )(act_all, cot_all)
        width = channels // parts
        own = lax.axis_index("dp") * width
        return grad, lax.dynamic_slice(gain, (0, own), (1, width))

    dec_weight_out, dec_gain_out = weight_grad(dec_act_all, dec_cot_all, DEC_TAPS)

    state = None
    for level in reversed(range(sections)):
        sent = []
        final = level == last
        for step in range(steps):
            skip = current[step] if final else skip_cots[level][step]
            (y,), state = staged_call(
                functools.partial(enc_backward_kernel, sizes, level, step, final),
                [current[step], skip, enc_taps, enc_gain, own_keep[0], spread_matrix, enc_xhat, enc_rstd],
                [row_shape],
                *back_state,
                state,
                cols,
                enc_flops,
            )
            sent.append(send(y, level, level - 1) if level > 0 else y)
        current = sent
    enc_cot_all = lax.all_gather(state[1], "dp")
    enc_weight_out, enc_gain_out = weight_grad(enc_act_all, enc_cot_all, ENC_TAPS)
    return (enc_weight_out[None], enc_gain_out, dec_weight_out[None], dec_gain_out)


def solution(mesh):
    placed = (
        P("dp", None, None, None, None),
        P("dp"),
        P("dp"),
        P("dp", None, None, None, None),
        P("dp", None),
        P("section", None, None),
        P("section", None),
        P("section", None, None),
        P("section", None),
    )
    return jax.shard_map(
        body,
        mesh=mesh,
        in_specs=placed,
        out_specs=(
            P("section", "dp", None),
            P("section", "dp"),
            P("section", "dp", None),
            P("section", "dp"),
        ),
        check_vma=False,
    )
```

time: 1040 us -> 720 us (0.69)
  waiting for transfers between devices: 408 us -> 2.97 us
  starting transfers between devices: 194 us -> 517 us
  other arithmetic: 209 us -> 4.18 us
  matrix products: 111 us -> 0 us
  Pallas kernels: 0 us -> 59.9 us
  blocking collectives: 0 us -> 29.6 us
    ppermute x66 -> x172, starting transfers between devices: 194 us -> 517 us  [send(): return lax.ppermute(value, 'section', [(source, target)])]
    ppermute x66 -> x172, waiting for transfers between devices: 300 us -> 2.93 us  [send(): return lax.ppermute(value, 'section', [(source, target)])]
    select_n x166 -> x1, other arithmetic: 127 us -> 0.66 us  [body(): clean = jnp.take(clip_pool, sample_ids, axis=0).astype(F32)]
    dot_general x34 -> x0, matrix products: 111 us -> none  [the longest x8 41.9 us: encoder_backward(): lax.dot_general(gated.reshape(-1, stream.shape[-1]), weight, (((1,), (1,)...]
    reduce_scatter x2 -> x0, waiting for transfers between devices: 101 us -> none  [the longest x1 66.1 us: body(): lax.psum_scatter(enc_weight_acc.astype(jnp.bfloat16), 'dp', scatter_dimen...]
    unnamed x24 -> x192, local copies, waits for them, and re-layouts: 3.66 us -> 67.8 us
    pallas_call x0 -> x131, Pallas kernels: none -> 59.9 us  [the longest x128 50.1 us: staged_call(): pl.pallas_call(kernel, in_specs=in_specs, out_specs=[VM] * (len(plain_out...]
    reduce_sum x184 -> x0, other arithmetic: 43.8 us -> none  [the longest x88 28.4 us: norm_act(): center = grouped - jnp.mean(grouped, axis=(1, 3), keepdims=True)]
  transfers between devices with their start and end apart: 70 -> 174, of which waited for: 61 -> 2; matrix products, arithmetic and copies ran while one was open for 17% -> 1% of each run, Pallas kernels for 0% -> 7%
where the time goes in v1:
time: 720 us; the launch traced here: 707 us
  starting transfers between devices  517 us (72%)
  local copies, waits for them, and re-layouts  75 us (10%)
  Pallas kernels  59.9 us (8%)
  blocking collectives  29.6 us (4%)
  between operations  18.9 us (3%)
    ppermute x172, starting transfers between devices, send(): return lax.ppermute(value, 'section', [(source, target)])  517 us
    unnamed x192, local copies, waits for them, and re-layouts  67.8 us
    pallas_call x128, Pallas kernels, staged_call(): pl.pallas_call(kernel, in_specs=in_specs, out_specs=[VM] * (len(plain_out...  50.1 us
    all_gather x1, blocking collectives, body(): enc_act_all = lax.all_gather(enc_act, 'dp')  15.5 us
  transfers between devices with their start and end apart: 174, of which 2 were waited for; matrix products, arithmetic and copies ran while one was open for 1% of the time, Pallas kernels for 7%

profile of v1, /device:TPU:0, one launch (start us, length us, event | category | flops | bytes accessed | tf_op | source)
XLA Modules:
  0.0 707.2 jit_solution(5964213132837043641)
XLA Ops:
  25.1 8.7 %collective-permute-start.3 = (bf16[48,640]{1,0:T(8,128)(2,1)}, bf16[48,640]{1,0:T(8,128)(2,1)}, u32[]{:S(2)}, u32[]{:S(2)}) collective-permute-start(bf16[48,640]{1,0:T(8,128)(2,1)} %get-tuple-element.495), channel_id=1, source_target_pairs={{0,4},{1,5},{2,6},{3,7}} | collective-permute-start | bytes 184328 | tf_op jit(solution)/shard_map/ppermute | solution.py:475
  120.0 7.4 %collective-permute-start.15 = (bf16[48,640]{1,0:T(8,128)(2,1)S(1)}, bf16[48,640]{1,0:T(8,128)(2,1)S(1)}, u32[]{:S(2)}, u32[]{:S(2)}) collective-permute-start(bf16[48,640]{1,0:T(8,128)(2,1)S(1)} %get-tuple-element.543), channel_id=1, source_target_pairs={{12,16},{13,17},{14,18},{15,19}} | collective-permute-start | bytes 184328 | tf_op jit(solution)/shard_map/ppermute | solution.py:475
  127.4 7.5 %collective-permute-start.14 = (bf16[48,640]{1,0:T(8,128)(2,1)S(1)}, bf16[48,640]{1,0:T(8,128)(2,1)S(1)}, u32[]{:S(2)}, u32[]{:S(2)}) collective-permute-start(bf16[48,640]{1,0:T(8,128)(2,1)S(1)} %get-tuple-element.542), channel_id=1, source_target_pairs={{12,16},{13,17},{14,18},{15,19}} | collective-permute-start | bytes 184328 | tf_op jit(solution)/shard_map/ppermute | solution.py:475
  137.8 16.1 %collective-permute-start.18 = (bf16[48,640]{1,0:T(8,128)(2,1)S(1)}, bf16[48,640]{1,0:T(8,128)(2,1)S(1)}, u32[]{:S(2)}, u32[]{:S(2)}) collective-permute-start(bf16[48,640]{1,0:T(8,128)(2,1)S(1)} %get-tuple-element.558), channel_id=1, source_target_pairs={{16,20},{17,21},{18,22},{19,23}} | collective-permute-start | bytes 184328 | tf_op jit(solution)/shard_map/ppermute | solution.py:475
  153.9 7.5 %collective-permute-start.17 = (bf16[48,640]{1,0:T(8,128)(2,1)S(1)}, bf16[48,640]{1,0:T(8,128)(2,1)S(1)}, u32[]{:S(2)}, u32[]{:S(2)}) collective-permute-start(bf16[48,640]{1,0:T(8,128)(2,1)S(1)} %get-tuple-element.557), channel_id=1, source_target_pairs={{16,20},{17,21},{18,22},{19,23}} | collective-permute-start | bytes 184328 | tf_op jit(solution)/shard_map/ppermute | solution.py:475
  170.8 30.0 %collective-permute-start.30 = (bf16[48,640]{1,0:T(8,128)(2,1)S(1)}, bf16[48,640]{1,0:T(8,128)(2,1)S(1)}, u32[]{:S(2)}, u32[]{:S(2)}) collective-permute-start(bf16[48,640]{1,0:T(8,128)(2,1)S(1)} %get-tuple-element.608), channel_id=1, source_target_pairs={{28,0},{29,1},{30,2},{31,3}} | collective-permute-start | bytes 184328 | tf_op jit(solution)/shard_map/ppermute | solution.py:475
  200.9 9.3 %collective-permute-start.29 = (bf16[48,640]{1,0:T(8,128)(2,1)S(1)}, bf16[48,640]{1,0:T(8,128)(2,1)S(1)}, u32[]{:S(2)}, u32[]{:S(2)}) collective-permute-start(bf16[48,640]{1,0:T(8,128)(2,1)S(1)} %get-tuple-element.607), channel_id=1, source_target_pairs={{28,0},{29,1},{30,2},{31,3}} | collective-permute-start | bytes 184328 | tf_op jit(solution)/shard_map/ppermute | solution.py:475
  253.6 8.4 %collective-permute-start.52 = (bf16[48,640]{1,0:T(8,128)(2,1)S(1)}, bf16[48,640]{1,0:T(8,128)(2,1)S(1)}, u32[]{:S(2)}, u32[]{:S(2)}) collective-permute-start(bf16[48,640]{1,0:T(8,128)(2,1)S(1)} %get-tuple-element.653), channel_id=1, source_target_pairs={{8,12},{9,13},{10,14},{11,15}} | collective-permute-start | bytes 184328 | tf_op jit(solution)/shard_map/ppermute | solution.py:475
  271.7 11.0 %collective-permute-start.58 = (bf16[48,640]{1,0:T(8,128)(2,1)S(1)}, bf16[48,640]{1,0:T(8,128)(2,1)S(1)}, u32[]{:S(2)}, u32[]{:S(2)}) collective-permute-start(bf16[48,640]{1,0:T(8,128)(2,1)S(1)} %get-tuple-element.669), channel_id=1, source_target_pairs={{12,16},{13,17},{14,18},{15,19}} | collective-permute-start | bytes 184328 | tf_op jit(solution)/shard_map/ppermute | solution.py:475
  286.9 10.7 %collective-permute-start.64 = (bf16[48,640]{1,0:T(8,128)(2,1)S(1)}, bf16[48,640]{1,0:T(8,128)(2,1)S(1)}, u32[]{:S(2)}, u32[]{:S(2)}) collective-permute-start(bf16[48,640]{1,0:T(8,128)(2,1)S(1)} %get-tuple-element.685), channel_id=1, source_target_pairs={{16,20},{17,21},{18,22},{19,23}} | collective-permute-start | bytes 184328 | tf_op jit(solution)/shard_map/ppermute | solution.py:475
  308.4 9.9 %collective-permute-start.72 = (bf16[48,640]{1,0:T(8,128)(2,1)S(1)}, bf16[48,640]{1,0:T(8,128)(2,1)S(1)}, u32[]{:S(2)}, u32[]{:S(2)}) collective-permute-start(bf16[48,640]{1,0:T(8,128)(2,1)S(1)} %get-tuple-element.701), channel_id=1, source_target_pairs={{20,24},{21,25},{22,26},{23,27}} | collective-permute-start | bytes 184328 | tf_op jit(solution)/shard_map/ppermute | solution.py:475
  364.1 8.3 %collective-permute-start.86 = (bf16[48,640]{1,0:T(8,128)(2,1)S(1)}, bf16[48,640]{1,0:T(8,128)(2,1)S(1)}, u32[]{:S(2)}, u32[]{:S(2)}) collective-permute-start(bf16[48,640]{1,0:T(8,128)(2,1)S(1)} %get-tuple-element.745), channel_id=1, source_target_pairs={{28,24},{29,25},{30,26},{31,27}} | collective-permute-start | bytes 184328 | tf_op jit(solution)/shard_map/ppermute | solution.py:475
  374.5 10.9 %collective-permute-start.91 = (bf16[48,640]{1,0:T(8,128)(2,1)S(1)}, bf16[48,640]{1,0:T(8,128)(2,1)S(1)}, u32[]{:S(2)}, u32[]{:S(2)}) collective-permute-start(bf16[48,640]{1,0:T(8,128)(2,1)S(1)} %get-tuple-element.758), channel_id=1, source_target_pairs={{24,20},{25,21},{26,22},{27,23}} | collective-permute-start | bytes 184328 | tf_op jit(solution)/shard_map/ppermute | solution.py:475
  386.1 7.4 %collective-permute-start.90 = (bf16[48,640]{1,0:T(8,128)(2,1)S(1)}, bf16[48,640]{1,0:T(8,128)(2,1)S(1)}, u32[]{:S(2)}, u32[]{:S(2)}) collective-permute-start(bf16[48,640]{1,0:T(8,128)(2,1)S(1)} %get-tuple-element.757), channel_id=1, source_target_pairs={{24,20},{25,21},{26,22},{27,23}} | collective-permute-start | bytes 184328 | tf_op jit(solution)/shard_map/ppermute | solution.py:475
  396.5 10.0 %collective-permute-start.95 = (bf16[48,640]{1,0:T(8,128)(2,1)S(1)}, bf16[48,640]{1,0:T(8,128)(2,1)S(1)}, u32[]{:S(2)}, u32[]{:S(2)}) collective-permute-start(bf16[48,640]{1,0:T(8,128)(2,1)S(1)} %get-tuple-element.770), channel_id=1, source_target_pairs={{20,16},{21,17},{22,18},{23,19}} | collective-permute-start | bytes 184328 | tf_op jit(solution)/shard_map/ppermute | solution.py:475
  406.6 7.4 %collective-permute-start.94 = (bf16[48,640]{1,0:T(8,128)(2,1)S(1)}, bf16[48,640]{1,0:T(8,128)(2,1)S(1)}, u32[]{:S(2)}, u32[]{:S(2)}) collective-permute-start(bf16[48,640]{1,0:T(8,128)(2,1)S(1)} %get-tuple-element.769), channel_id=1, source_target_pairs={{20,16},{21,17},{22,18},{23,19}} | collective-permute-start | bytes 184328 | tf_op jit(solution)/shard_map/ppermute | solution.py:475
  420.9 13.5 %collective-permute-start.103 = (bf16[48,640]{1,0:T(8,128)(2,1)S(1)}, bf16[48,640]{1,0:T(8,128)(2,1)S(1)}, u32[]{:S(2)}, u32[]{:S(2)}) collective-permute-start(bf16[48,640]{1,0:T(8,128)(2,1)S(1)} %get-tuple-element.794), channel_id=1, source_target_pairs={{12,8},{13,9},{14,10},{15,11}} | collective-permute-start | bytes 184328 | tf_op jit(solution)/shard_map/ppermute | solution.py:475
  443.7 9.0 %collective-permute-start.107 = (bf16[48,640]{1,0:T(8,128)(2,1)S(1)}, bf16[48,640]{1,0:T(8,128)(2,1)S(1)}, u32[]{:S(2)}, u32[]{:S(2)}) collective-permute-start(bf16[48,640]{1,0:T(8,128)(2,1)S(1)} %get-tuple-element.806), channel_id=1, source_target_pairs={{8,4},{9,5},{10,6},{11,7}} | collective-permute-start | bytes 184328 | tf_op jit(solution)/shard_map/ppermute | solution.py:475
  461.7 8.2 %collective-permute-start.111 = (bf16[48,640]{1,0:T(8,128)(2,1)S(1)}, bf16[48,640]{1,0:T(8,128)(2,1)S(1)}, u32[]{:S(2)}, u32[]{:S(2)}) collective-permute-start(bf16[48,640]{1,0:T(8,128)(2,1)S(1)} %get-tuple-element.818), channel_id=1, source_target_pairs={{4,0},{5,1},{6,2},{7,3}} | collective-permute-start | bytes 184328 | tf_op jit(solution)/shard_map/ppermute | solution.py:475
  499.0 7.2 %collective-permute-start.113 = (bf16[48,640]{1,0:T(8,128)(2,1)}, bf16[48,640]{1,0:T(8,128)(2,1)S(1)}, u32[]{:S(2)}, u32[]{:S(2)}) collective-permute-start(bf16[48,640]{1,0:T(8,128)(2,1)} %copy-done.93), channel_id=1, source_target_pairs={{0,28},{1,29},{2,30},{3,31}} | collective-permute-start | bytes 184328 | tf_op jit(solution)/shard_map/ppermute | solution.py:475
  566.0 50.4 %collective-permute-start.169 = (bf16[48,640]{1,0:T(8,128)(2,1)S(1)}, bf16[48,640]{1,0:T(8,128)(2,1)S(1)}, u32[]{:S(2)}, u32[]{:S(2)}) collective-permute-start(bf16[48,640]{1,0:T(8,128)(2,1)S(1)} %copy-done.43), channel_id=1, source_target_pairs={{28,0},{29,1},{30,2},{31,3}} | collective-permute-start | bytes 184328 | tf_op jit(solution)/shard_map/ppermute | solution.py:475
  633.9 7.4 %collective-permute-start.166 = (bf16[48,640]{1,0:T(8,128)(2,1)S(1)}, bf16[48,640]{1,0:T(8,128)(2,1)S(1)}, u32[]{:S(2)}, u32[]{:S(2)}) collective-permute-start(bf16[48,640]{1,0:T(8,128)(2,1)S(1)} %get-tuple-element.937), channel_id=1, source_target_pairs={{4,0},{5,1},{6,2},{7,3}} | collective-permute-start | bytes 184328 | tf_op jit(solution)/shard_map/ppermute | solution.py:475
  658.4 15.5 %all-gather = bf16[768,640]{1,0:T(8,128)(2,1)S(1)} all-gather(bf16[192,640]{1,0:T(8,128)(2,1)S(1)} %copy-done.28), channel_id=2, replica_groups=mesh['section'=8,'dp'=4] {'dp'}, dimensions={0}, use_global_device_ids=true | all-gather | bytes 1228800 | tf_op jit(solution)/shard_map/all_gather | solution.py:500
  673.9 14.1 %all-gather.2 = bf16[768,640]{1,0:T(8,128)(2,1)S(1)} all-gather(bf16[192,640]{1,0:T(8,128)(2,1)S(1)} %copy-done.20), channel_id=4, replica_groups=mesh['section'=8,'dp'=4] {'dp'}, dimensions={0}, use_global_device_ids=true | all-gather | bytes 1228800 | tf_op jit(solution)/shard_map/all_gather | solution.py:520
  (668 shorter events, 392.3 us)
Async XLA Ops:
  7.2 680.8 %all-gather.9.cloned.1.call-start = ((), (), s32[]{:S(2)}) async-start(), calls=%async_computation.1 | async-start | bytes 1331200 | tf_op jit(solution)/shard_map/all_gather | solution.py:543
  25.1 54.4 %collective-permute-start.3 = (bf16[48,640]{1,0:T(8,128)(2,1)}, bf16[48,640]{1,0:T(8,128)(2,1)}, u32[]{:S(2)}, u32[]{:S(2)}) collective-permute-start(bf16[48,640]{1,0:T(8,128)(2,1)} %get-tuple-element.495), channel_id=1, source_target_pairs={{0,4},{1,5},{2,6},{3,7}} | collective-permute-start | bytes 184328 | tf_op jit(solution)/shard_map/ppermute | solution.py:475
  33.8 135.0 %collective-permute-start.83 = (bf16[48,640]{1,0:T(8,128)(2,1)}, bf16[48,640]{1,0:T(8,128)(2,1)}, u32[]{:S(2)}, u32[]{:S(2)}) collective-permute-start(bf16[48,640]{1,0:T(8,128)(2,1)} %get-tuple-element.495), channel_id=1, source_target_pairs={{0,28},{1,29},{2,30},{3,31}} | collective-permute-start | bytes 184328 | tf_op jit(solution)/shard_map/ppermute | solution.py:475
  50.7 32.4 %collective-permute-start.2 = (bf16[48,640]{1,0:T(8,128)(2,1)}, bf16[48,640]{1,0:T(8,128)(2,1)}, u32[]{:S(2)}, u32[]{:S(2)}) collective-permute-start(bf16[48,640]{1,0:T(8,128)(2,1)} %get-tuple-element.494), channel_id=1, source_target_pairs={{0,4},{1,5},{2,6},{3,7}} | collective-permute-start | bytes 184328 | tf_op jit(solution)/shard_map/ppermute | solution.py:475
  64.6 25.9 %collective-permute-start.1 = (bf16[48,640]{1,0:T(8,128)(2,1)}, bf16[48,640]{1,0:T(8,128)(2,1)}, u32[]{:S(2)}, u32[]{:S(2)}) collective-permute-start(bf16[48,640]{1,0:T(8,128)(2,1)} %get-tuple-element.493), channel_id=1, source_target_pairs={{0,4},{1,5},{2,6},{3,7}} | collective-permute-start | bytes 184328 | tf_op jit(solution)/shard_map/ppermute | solution.py:475
  136.4 25.0 %collective-permute-start.19 = (bf16[48,640]{1,0:T(8,128)(2,1)S(1)}, bf16[48,640]{1,0:T(8,128)(2,1)S(1)}, u32[]{:S(2)}, u32[]{:S(2)}) collective-permute-start(bf16[48,640]{1,0:T(8,128)(2,1)S(1)} %get-tuple-element.559), channel_id=1, source_target_pairs={{16,20},{17,21},{18,22},{19,23}} | collective-permute-start | bytes 184328 | tf_op jit(solution)/shard_map/ppermute | solution.py:475
  137.1 32.4 %collective-permute-start.55 = (bf16[48,640]{1,0:T(8,128)(2,1)S(1)}, bf16[48,640]{1,0:T(8,128)(2,1)S(1)}, u32[]{:S(2)}, u32[]{:S(2)}) collective-permute-start(bf16[48,640]{1,0:T(8,128)(2,1)S(1)} %get-tuple-element.559), channel_id=1, source_target_pairs={{16,12},{17,13},{18,14},{19,15}} | collective-permute-start | bytes 184328 | tf_op jit(solution)/shard_map/ppermute | solution.py:475
  137.8 24.4 %collective-permute-start.18 = (bf16[48,640]{1,0:T(8,128)(2,1)S(1)}, bf16[48,640]{1,0:T(8,128)(2,1)S(1)}, u32[]{:S(2)}, u32[]{:S(2)}) collective-permute-start(bf16[48,640]{1,0:T(8,128)(2,1)S(1)} %get-tuple-element.558), channel_id=1, source_target_pairs={{16,20},{17,21},{18,22},{19,23}} | collective-permute-start | bytes 184328 | tf_op jit(solution)/shard_map/ppermute | solution.py:475
  162.9 47.5 %collective-permute-start.47 = (bf16[48,640]{1,0:T(8,128)(2,1)S(1)}, bf16[48,640]{1,0:T(8,128)(2,1)S(1)}, u32[]{:S(2)}, u32[]{:S(2)}) collective-permute-start(bf16[48,640]{1,0:T(8,128)(2,1)S(1)} %get-tuple-element.575), channel_id=1, source_target_pairs={{20,8},{21,9},{22,10},{23,11}} | collective-permute-start | bytes 184328 | tf_op jit(solution)/shard_map/ppermute | solution.py:475
  168.1 32.8 %collective-permute-start.24 = (bf16[48,640]{1,0:T(8,128)(2,1)S(1)}, bf16[48,640]{1,0:T(8,128)(2,1)S(1)}, u32[]{:S(2)}, u32[]{:S(2)}) collective-permute-start(bf16[48,640]{1,0:T(8,128)(2,1)S(1)} %get-tuple-element.588), channel_id=1, source_target_pairs={{24,28},{25,29},{26,30},{27,31}} | collective-permute-start | bytes 184328 | tf_op jit(solution)/shard_map/ppermute | solution.py:475
  168.8 44.7 %collective-permute-start.45 = (bf16[48,640]{1,0:T(8,128)(2,1)S(1)}, bf16[48,640]{1,0:T(8,128)(2,1)S(1)}, u32[]{:S(2)}, u32[]{:S(2)}) collective-permute-start(bf16[48,640]{1,0:T(8,128)(2,1)S(1)} %get-tuple-element.574), channel_id=1, source_target_pairs={{20,8},{21,9},{22,10},{23,11}} | collective-permute-start | bytes 184328 | tf_op jit(solution)/shard_map/ppermute | solution.py:475
  169.5 41.5 %collective-permute-start.31 = (bf16[48,640]{1,0:T(8,128)(2,1)S(1)}, bf16[48,640]{1,0:T(8,128)(2,1)S(1)}, u32[]{:S(2)}, u32[]{:S(2)}) collective-permute-start(bf16[48,640]{1,0:T(8,128)(2,1)S(1)} %get-tuple-element.609), channel_id=1, source_target_pairs={{28,0},{29,1},{30,2},{31,3}} | collective-permute-start | bytes 184328 | tf_op jit(solution)/shard_map/ppermute | solution.py:475
  170.8 43.4 %collective-permute-start.30 = (bf16[48,640]{1,0:T(8,128)(2,1)S(1)}, bf16[48,640]{1,0:T(8,128)(2,1)S(1)}, u32[]{:S(2)}, u32[]{:S(2)}) collective-permute-start(bf16[48,640]{1,0:T(8,128)(2,1)S(1)} %get-tuple-element.608), channel_id=1, source_target_pairs={{28,0},{29,1},{30,2},{31,3}} | collective-permute-start | bytes 184328 | tf_op jit(solution)/shard_map/ppermute | solution.py:475
  320.4 23.6 %collective-permute-start.81 = (bf16[48,640]{1,0:T(8,128)(2,1)}, bf16[48,640]{1,0:T(8,128)(2,1)S(1)}, u32[]{:S(2)}, u32[]{:S(2)}) collective-permute-start(bf16[48,640]{1,0:T(8,128)(2,1)} %get-tuple-element.494), channel_id=1, source_target_pairs={{0,28},{1,29},{2,30},{3,31}} | collective-permute-start | bytes 184328 | tf_op jit(solution)/shard_map/ppermute | solution.py:475
  328.5 25.7 %collective-permute-start.80 = (bf16[48,640]{1,0:T(8,128)(2,1)}, bf16[48,640]{1,0:T(8,128)(2,1)}, u32[]{:S(2)}, u32[]{:S(2)}) collective-permute-start(bf16[48,640]{1,0:T(8,128)(2,1)} %get-tuple-element.717), channel_id=1, source_target_pairs={{24,28},{25,29},{26,30},{27,31}} | collective-permute-start | bytes 184328 | tf_op jit(solution)/shard_map/ppermute | solution.py:475
  419.5 22.7 %collective-permute-start.96 = (bf16[48,640]{1,0:T(8,128)(2,1)S(1)}, bf16[48,640]{1,0:T(8,128)(2,1)S(1)}, u32[]{:S(2)}, u32[]{:S(2)}) collective-permute-start(bf16[48,640]{1,0:T(8,128)(2,1)S(1)} %get-tuple-element.779), channel_id=1, source_target_pairs={{16,12},{17,13},{18,14},{19,15}} | collective-permute-start | bytes 184328 | tf_op jit(solution)/shard_map/ppermute | solution.py:475
  461.7 23.1 %collective-permute-start.111 = (bf16[48,640]{1,0:T(8,128)(2,1)S(1)}, bf16[48,640]{1,0:T(8,128)(2,1)S(1)}, u32[]{:S(2)}, u32[]{:S(2)}) collective-permute-start(bf16[48,640]{1,0:T(8,128)(2,1)S(1)} %get-tuple-element.818), channel_id=1, source_target_pairs={{4,0},{5,1},{6,2},{7,3}} | collective-permute-start | bytes 184328 | tf_op jit(solution)/shard_map/ppermute | solution.py:475
  493.7 198.8 %all-gather.7.cloned.1.call-start = ((), (), s32[]{:S(2)}) async-start(), calls=%async_computation | async-start | bytes 1331200 | tf_op jit(solution)/shard_map/all_gather | solution.py:587
  496.3 136.3 %collective-permute-start.171 = (bf16[48,640]{1,0:T(8,128)(2,1)}, bf16[48,640]{1,0:T(8,128)(2,1)S(1)}, u32[]{:S(2)}, u32[]{:S(2)}) collective-permute-start(bf16[48,640]{1,0:T(8,128)(2,1)} %copy-done.44), channel_id=1, source_target_pairs={{28,0},{29,1},{30,2},{31,3}} | collective-permute-start | bytes 184328 | tf_op jit(solution)/shard_map/ppermute | solution.py:475
  562.3 54.0 %collective-permute-start.158 = (bf16[48,640]{1,0:T(8,128)(2,1)S(1)}, bf16[48,640]{1,0:T(8,128)(2,1)S(1)}, u32[]{:S(2)}, u32[]{:S(2)}) collective-permute-start(bf16[48,640]{1,0:T(8,128)(2,1)S(1)} %get-tuple-element.921), channel_id=1, source_target_pairs={{8,4},{9,5},{10,6},{11,7}} | collective-permute-start | bytes 184328 | tf_op jit(solution)/shard_map/ppermute | solution.py:475
  563.8 53.9 %collective-permute-start.157 = (bf16[48,640]{1,0:T(8,128)(2,1)S(1)}, bf16[48,640]{1,0:T(8,128)(2,1)S(1)}, u32[]{:S(2)}, u32[]{:S(2)}) collective-permute-start(bf16[48,640]{1,0:T(8,128)(2,1)S(1)} %copy-done.46), channel_id=1, source_target_pairs={{24,4},{25,5},{26,6},{27,7}} | collective-permute-start | bytes 184328 | tf_op jit(solution)/shard_map/ppermute | solution.py:475
  564.5 61.1 %collective-permute-start.156 = (bf16[48,640]{1,0:T(8,128)(2,1)S(1)}, bf16[48,640]{1,0:T(8,128)(2,1)S(1)}, u32[]{:S(2)}, u32[]{:S(2)}) collective-permute-start(bf16[48,640]{1,0:T(8,128)(2,1)S(1)} %get-tuple-element.919), channel_id=1, source_target_pairs={{8,4},{9,5},{10,6},{11,7}} | collective-permute-start | bytes 184328 | tf_op jit(solution)/shard_map/ppermute | solution.py:475
  566.0 79.1 %collective-permute-start.169 = (bf16[48,640]{1,0:T(8,128)(2,1)S(1)}, bf16[48,640]{1,0:T(8,128)(2,1)S(1)}, u32[]{:S(2)}, u32[]{:S(2)}) collective-permute-start(bf16[48,640]{1,0:T(8,128)(2,1)S(1)} %copy-done.43), channel_id=1, source_target_pairs={{28,0},{29,1},{30,2},{31,3}} | collective-permute-start | bytes 184328 | tf_op jit(solution)/shard_map/ppermute | solution.py:475
  618.5 31.7 %collective-permute-start.167 = (bf16[48,640]{1,0:T(8,128)(2,1)S(1)}, bf16[48,640]{1,0:T(8,128)(2,1)S(1)}, u32[]{:S(2)}, u32[]{:S(2)}) collective-permute-start(bf16[48,640]{1,0:T(8,128)(2,1)S(1)} %copy-done.41), channel_id=1, source_target_pairs={{28,0},{29,1},{30,2},{31,3}} | collective-permute-start | bytes 184328 | tf_op jit(solution)/shard_map/ppermute | solution.py:475
  (246 other events, 1935.6 us)
Sparse Core Ops, SparseCore 0:
  493.8 14.0 all-gather.8
  658.5 17.8 all-gather.6
